TPU v7x, 32 devices: a whole 2x2x4 slice. The times are simulated.
32 devices in a mesh: dp: 8 (over y, x, core), tensor: 4 (over z).
Axes of the slice: x: 2, y: 2, z: 4, core: 2. Of those that a mesh axis runs over, the one named last changes fastest.
Arguments:
- out_grad: bfloat16 [8, 256, 4096], P('dp', 'tensor'), may hold values from -6 to 6
- out_weight: bfloat16 [4096, 1024], P('dp', 'tensor'), may hold values from -0.1875 to 0.1875
- queries: bfloat16 [8, 256, 1024], P('dp', None, 'tensor'), may hold values from -5 to 5
- keys: bfloat16 [8, 256, 512], P('dp', None, 'tensor'), may hold values from -5 to 5, as said below
- values: bfloat16 [8, 256, 512], P('dp', None, 'tensor'), may hold values from -6 to 6, as said below
- segment_ids: int32 [8, 256], P('dp'), may hold values from 0 to 3, never falling along the last dimension, each value on 1 to 128 neighbouring positions
Outputs:
- d_queries: bfloat16 [8, 256, 1024], P('dp', None, 'tensor')
- d_keys: bfloat16 [8, 256, 512], P('dp', None, 'tensor')
- d_values: bfloat16 [8, 256, 512], P('dp', None, 'tensor')
- d_out_weight: float32 [4096, 1024], P('dp', 'tensor')
Inputs may be any that keep to these rules, and one draw needn't show every extreme that they name: `keys`: column blocks 2 g and 2 g + 1 are equal. `values`: column blocks 2 g and 2 g + 1 are equal.
All inputs are finite; a program needn't handle non-finite values.
Results may differ from a plain program's by a relative error of at most 0.018.
Values may be sent and summed in bfloat16 or wider, within the bound.
A program may use at most 128 MiB of HBM per device.

v0:
```python
import jax
import jax.numpy as jnp
from jax import lax
from jax.sharding import PartitionSpec as P

HD = 128


def from_partner(block, axis, bit):
    count = lax.axis_size(axis)
    route = []
    for low in range(count):
        high = low | 1 << bit
        if high != low and high < count:
            route += [(low, high), (high, low)]
    return lax.ppermute(block, axis, route)


def local(out_grad, out_weight, queries, keys, values, segment_ids):
    scale = HD ** (-0.5)
    grad_local = out_grad[0]
    query_rows = queries[0]
    length = query_rows.shape[0]
    width = query_rows.shape[1]
    heads_here = width // HD
    key_local = keys[0]
    value_local = values[0]
    query_heads = query_rows.reshape(length, heads_here, HD)
    scores = (
        jnp.einsum("qhd,kd->hqk", query_heads, key_local, preferred_element_type=jnp.float32)
        * scale
    )
    segments = segment_ids[0]
    position = jnp.arange(length)
    visible = (segments[:, None] == segments[None, :]) & (position[:, None] >= position[None, :])
    masked = jnp.where(visible[None], scores, -jnp.inf)
    top_score = jnp.max(masked, axis=-1, keepdims=True)
    raw_exp = jnp.exp(masked - top_score)
    attn_prob = raw_exp / jnp.sum(raw_exp, axis=-1, keepdims=True)
    prob_low = attn_prob.astype(jnp.bfloat16)
    attn_out = jnp.einsum(
        "hqk,kd->qhd", prob_low, value_local, preferred_element_type=jnp.float32
    ).astype(jnp.bfloat16)
    flat_out = attn_out.reshape(length, width)
    grad_full = lax.all_gather(grad_local, "tensor", axis=0, tiled=True)
    columns = grad_full
    grad_sum = jnp.dot(
        columns,
        lax.all_gather(out_weight, "dp", axis=0, tiled=True),
        preferred_element_type=jnp.float32,
    )
    columns = grad_full
    weight_rows = lax.psum_scatter(
        lax.dot_general(
            columns, flat_out, (((0,), (0,)), ((), ())), preferred_element_type=jnp.float32
        ).astype(jnp.bfloat16),
        "dp",
        scatter_dimension=0,
        tiled=True,
    ).astype(jnp.float32)
    grad_attn = grad_sum.astype(jnp.bfloat16)
    grad_heads = grad_attn.reshape(length, heads_here, HD)
    deltas = jnp.sum(grad_heads.astype(jnp.float32) * attn_out.astype(jnp.float32), axis=-1)
    grad_values = jnp.einsum(
        "hqk,qhd->kd", prob_low, grad_heads, preferred_element_type=jnp.float32
    )
    grad_prob = jnp.einsum(
        "qhd,kd->hqk", grad_heads, value_local, preferred_element_type=jnp.float32
    )
    grad_score = (attn_prob * (grad_prob - jnp.transpose(deltas)[:, :, None]) * scale).astype(
        jnp.bfloat16
    )
    grad_queries = jnp.einsum(
        "hqk,kd->qhd", grad_score, key_local, preferred_element_type=jnp.float32
    ).astype(jnp.bfloat16)
    grad_keys = jnp.einsum(
        "hqk,qhd->kd", grad_score, query_heads, preferred_element_type=jnp.float32
    )
    partner_keys, partner_values = (
        from_partner(grad_keys.astype(jnp.bfloat16), "tensor", 0).astype(grad_keys.dtype),
        from_partner(grad_values.astype(jnp.bfloat16), "tensor", 0).astype(grad_values.dtype),
    )
    keys_total = (grad_keys + partner_keys).astype(jnp.bfloat16)
    values_total = (grad_values + partner_values).astype(jnp.bfloat16)
    weight_grad = weight_rows / lax.axis_size("dp")
    return (
        grad_queries.reshape(1, length, width),
        keys_total[None],
        values_total[None],
        weight_grad,
    )


def solution(mesh):
    in_specs = (
        P("dp", "tensor", None),
        P("dp", "tensor"),
        P("dp", None, "tensor"),
        P("dp", None, "tensor"),
        P("dp", None, "tensor"),
        P("dp", None),
    )
    out_specs = (
        P("dp", None, "tensor"),
        P("dp", None, "tensor"),
        P("dp", None, "tensor"),
        P("dp", "tensor"),
    )
    return jax.shard_map(local, mesh=mesh, in_specs=in_specs, out_specs=out_specs, check_vma=False)
```

profile of v0, /device:TPU:0, one launch (start us, length us, event | category | flops | bytes accessed | tf_op | source)
XLA Modules:
  0.0 143.6 jit_solution(18421356278678418032)
XLA Ops:
  7.2 0.0 copy-start
  7.2 0.0 all-gather.6.cloned.1.call-start
  7.2 0.7 all-gather.6.cloned.1.call-update
  7.9 0.0 all-gather.4.cloned.1.call-start
  8.0 0.7 all-gather.4.cloned.1.call-update
  8.7 0.0 reduce-scatter.2.cloned.1.call-start
  8.7 0.9 reshape_squeeze.3
  9.7 0.9 fusion.16
  10.5 0.0 copy-done
  10.5 0.3 fusion.55
  10.9 47.4 %all-gather.6.cloned.1.call-done = bf16[1,256,4096]{2,1,0:T(8,128)(2,1)} async-done(((bf16[1,64,4096]{2,1,0:T(8,128)(2,1)}), bf16[1,256,4096]{2,1,0:T(8,128)(2,1)}) %all-gather.6.cloned.1.call-update) | async-done | bytes 2097168 | tf_op jit(solution)/shard_map/all_gather | solution.py:45
  58.3 28.5 %all-gather.4.cloned.1.call-done = bf16[4096,256]{1,0:T(8,128)(2,1)} async-done(((bf16[512,256]{1,0:T(8,128)(2,1)}), bf16[4096,256]{1,0:T(8,128)(2,1)}) %all-gather.4.cloned.1.call-update) | async-done | bytes 2097168 | tf_op jit(solution)/shard_map/all_gather | solution.py:49
  86.8 3.1 %fusion.13 = bf16[256,256]{0,1:T(8,128)(2,1)S(1)} fusion(bf16[4096,256]{1,0:T(8,128)(2,1)} %all-gather.4.cloned.1.call-done, bf16[1,256,4096]{2,1,0:T(8,128)(2,1)} %all-gather.6.cloned.1.call-done), kind=kOutput, calls=%fused_computation.18 | convolution fusion | flops 536936448 | bytes 4325376 | tf_op jit(solution)/shard_map/dot_general | solution.py:47
  89.9 0.0 copy-start.1
  90.0 0.5 multiply_reduce_fusion
  90.5 1.0 copy-done.1
  91.5 2.1 %fusion.1 = bf16[4096,256]{0,1:T(8,128)(2,1)} fusion(bf16[256,256]{0,1:T(8,128)(2,1)S(1)} %bitcast.105, bf16[1,256,4096]{2,1,0:T(8,128)(2,1)S(1)} %copy-done.1), kind=kOutput, calls=%fused_computation.2 | convolution fusion | flops 537919488 | bytes 4325376 | tf_op jit(solution)/shard_map/dot_general | solution.py:54
  93.6 0.0 reduce-scatter.2.cloned.1.call-update
  93.6 0.2 fusion.12
  93.8 0.2 fusion.64
  94.1 1.5 %collective-permute-start = (bf16[256,128]{1,0:T(8,128)(2,1)S(1)}, bf16[256,128]{1,0:T(8,128)(2,1)S(1)}, u32[]{:S(2)}, u32[]{:S(2)}) collective-permute-start(bf16[256,128]{1,0:T(8,128)(2,1)S(1)} %get-tuple-element.12), channel_id=1, source_target_pairs={{0,1},{1,0},{2,3},{3,2},{4,5},{5,4},{6,7},{7,6},{8,9},{9,8},{10,11... | collective-permute-start | bytes 196616 | tf_op jit(solution)/shard_map/ppermute | solution.py:16
  95.6 0.2 convolution_convert_fusion.1
  95.8 0.5 fusion.65
  96.4 0.8 copy.19
  97.1 0.5 collective-permute-start.1
  97.7 0.7 collective-permute-done
  98.4 0.6 fusion.20
  99.0 2.3 %collective-permute-done.1 = bf16[256,128]{1,0:T(8,128)(2,1)S(1)} collective-permute-done((bf16[256,128]{1,0:T(8,128)(2,1)S(1)}, bf16[256,128]{1,0:T(8,128)(2,1)S(1)}, u32[]{:S(2)}, u32[]{:S(2)}) %collective-permute-start.1) | collective-permute-done | bytes 65568 | tf_op jit(solution)/shard_map/ppermute | solution.py:16
  101.4 0.6 fusion.21
  102.0 33.0 %reduce-scatter.2.cloned.1.call-done = bf16[512,256]{0,1:T(8,128)(2,1)} async-done(((bf16[4096,256]{0,1:T(8,128)(2,1)}), bf16[512,256]{0,1:T(8,128)(2,1)}) %reduce-scatter.2.cloned.1.call-update) | async-done | bytes 262160 | tf_op jit(solution)/shard_map/reduce_scatter | solution.py:53
  135.0 1.0 convert_multiply_fusion
  136.0 1.0 copy.20
  (2 shorter events, 0.0 us)
Async XLA Ops:
  7.2 3.4 %copy-start = (bf16[1,256,128]{2,1,0:T(8,128)(2,1)S(1)}, bf16[1,256,128]{2,1,0:T(8,128)(2,1)}, u32[]{:S(2)}) copy-start(bf16[1,256,128]{2,1,0:T(8,128)(2,1)} %param.9) | copy-start | bytes 196612
  7.2 51.1 %all-gather.6.cloned.1.call-start = ((), (), s32[]{:S(2)}) async-start(), calls=%async_computation.3 | async-start | bytes 2621440 | tf_op jit(solution)/shard_map/all_gather | solution.py:45
  7.9 78.9 %all-gather.4.cloned.1.call-start = ((), (), s32[]{:S(2)}) async-start(), calls=%async_computation.1 | async-start | bytes 2359296 | tf_op jit(solution)/shard_map/all_gather | solution.py:49
  8.7 126.3 %reduce-scatter.2.cloned.1.call-start = ((), (), s32[]{:S(2)}) async-start(), calls=%async_computation.2 | async-start | bytes 2359296 | tf_op jit(solution)/shard_map/reduce_scatter | solution.py:53
  10.9 79.1 %copy-start.2 = (bf16[1,256,128]{2,1,0:T(8,128)(2,1)S(1)}, bf16[1,256,128]{2,1,0:T(8,128)(2,1)}, u32[]{:S(2)}) copy-start(bf16[1,256,128]{2,1,0:T(8,128)(2,1)} %param.10) | copy-start | bytes 196612
  89.9 1.6 %copy-start.1 = (bf16[1,256,4096]{2,1,0:T(8,128)(2,1)S(1)}, bf16[1,256,4096]{2,1,0:T(8,128)(2,1)}, u32[]{:S(2)}) copy-start(bf16[1,256,4096]{2,1,0:T(8,128)(2,1)} %all-gather.6.cloned.1.call-done) | copy-start | bytes 6291460
  94.1 4.3 %collective-permute-start = (bf16[256,128]{1,0:T(8,128)(2,1)S(1)}, bf16[256,128]{1,0:T(8,128)(2,1)S(1)}, u32[]{:S(2)}, u32[]{:S(2)}) collective-permute-start(bf16[256,128]{1,0:T(8,128)(2,1)S(1)} %get-tuple-element.12), channel_id=1, source_target_pairs={{0,1},{1,0},{2,3},{3,2},{4,5},{5,4},{6,7},{7,6},{8,9},{9,8},{10,11... | collective-permute-start | bytes 196616 | tf_op jit(solution)/shard_map/ppermute | solution.py:16
  97.1 4.3 %collective-permute-start.1 = (bf16[256,128]{1,0:T(8,128)(2,1)S(1)}, bf16[256,128]{1,0:T(8,128)(2,1)S(1)}, u32[]{:S(2)}, u32[]{:S(2)}) collective-permute-start(bf16[256,128]{1,0:T(8,128)(2,1)S(1)} %get-tuple-element.14), channel_id=1, source_target_pairs={{0,1},{1,0},{2,3},{3,2},{4,5},{5,4},{6,7},{7,6},{8,9},{9,8},{10,11... | collective-permute-start | bytes 196616 | tf_op jit(solution)/shard_map/ppermute | solution.py:16
Sparse Core Ops, SparseCore 0:
  9.6 48.6 all-gather.5
  60.1 26.5 all-gather.3
  93.7 41.2 reduce-scatter.1
where the time goes:
time: 144 us
  waiting for transfers between devices  113 us (78%)
  between operations  13.8 us (10%)
  matrix products  7.24 us (5%)
  local copies, waits for them, and re-layouts  3.77 us (3%)
  other arithmetic  3.15 us (2%)
  starting transfers between devices  2.2 us (2%)
    all_gather x1, waiting for transfers between devices, local(): grad_full = lax.all_gather(grad_local, 'tensor', axis=0, tiled=True)  47.4 us
    reduce_scatter x1, waiting for transfers between devices, local(): lax.psum_scatter(lax.dot_general(columns, flat_out, (((0,), (0,)), ((), (...  33 us
    all_gather x1, waiting for transfers between devices, local(): lax.all_gather(out_weight, 'dp', axis=0, tiled=True)  28.5 us
    dot_general x1, matrix products, local(): jnp.dot(columns, lax.all_gather(out_weight, 'dp', axis=0, tiled=True), pr...  3.15 us
    ppermute x2, waiting for transfers between devices, from_partner(): return lax.ppermute(block, axis, route)  3.08 us
  transfers between devices with their start and end apart: 5, of which 5 were waited for; matrix products, arithmetic and copies ran while one was open for 4% of the time, Pallas kernels for 0%

commit v1 on v0

--- a/solution.py
+++ b/solution.py
@@ -42,7 +42,14 @@
         "hqk,kd->qhd", prob_low, value_local, preferred_element_type=jnp.float32
     ).astype(jnp.bfloat16)
     flat_out = attn_out.reshape(length, width)
-    grad_full = lax.all_gather(grad_local, "tensor", axis=0, tiled=True)
+    ring = [grad_local]
+    for hop in range(3):
+        ring.append(lax.ppermute(ring[-1], "tensor", [(dev, (dev + 1) % 4) for dev in range(4)]))
+    grad_full = jnp.roll(
+        jnp.concatenate(ring[::-1], axis=0),
+        (lax.axis_index("tensor") + 1) * ring[0].shape[0],
+        axis=0,
+    )
     columns = grad_full
     grad_sum = jnp.dot(
         columns,

time: 144 us -> 126 us (0.88)
  waiting for transfers between devices: 113 us -> 85.4 us
  local copies, waits for them, and re-layouts: 3.77 us -> 8.42 us
  starting transfers between devices: 2.2 us -> 5.32 us
  matrix products: 7.24 us -> 8.86 us
    all_gather x1 -> x0, waiting for transfers between devices: 47.4 us -> none  [local(): grad_full = lax.all_gather(grad_local, 'tensor', axis=0, tiled=True)]
    ppermute x0 -> x3, waiting for transfers between devices: none -> 40.8 us  [local(): lax.ppermute(ring[-1], 'tensor', [(dev, (dev + 1) % 4) for dev in range(4)])]
    all_gather x1, waiting for transfers between devices: 28.5 us -> 8.6 us  [local(): lax.all_gather(out_weight, 'dp', axis=0, tiled=True)]
    unnamed x8 -> x14, local copies, waits for them, and re-layouts: 2.83 us -> 6.63 us
    ppermute x0 -> x3, starting transfers between devices: none -> 3.08 us  [local(): lax.ppermute(ring[-1], 'tensor', [(dev, (dev + 1) % 4) for dev in range(4)])]
    dot_general x1, matrix products: 2.06 us -> 3.69 us  [local(): lax.dot_general(columns, flat_out, (((0,), (0,)), ((), ())), preferred_el...]
  transfers between devices with their start and end apart: 5 -> 7, of which waited for: 5 -> 7; matrix products, arithmetic and copies ran while one was open for 4% -> 10% of each run, Pallas kernels for 0% -> 0%
where the time goes in v1:
time: 126 us
  waiting for transfers between devices  85.4 us (68%)
  between operations  14.2 us (11%)
  matrix products  8.86 us (7%)
  local copies, waits for them, and re-layouts  8.42 us (7%)
  starting transfers between devices  5.32 us (4%)
  other arithmetic  3.93 us (3%)
    ppermute x3, waiting for transfers between devices, local(): lax.ppermute(ring[-1], 'tensor', [(dev, (dev + 1) % 4) for dev in range(4)])  40.8 us
    reduce_scatter x1, waiting for transfers between devices, local(): lax.psum_scatter(lax.dot_general(columns, flat_out, (((0,), (0,)), ((), (...  33.6 us
    all_gather x1, waiting for transfers between devices, local(): lax.all_gather(out_weight, 'dp', axis=0, tiled=True)  8.6 us
    unnamed x14, local copies, waits for them, and re-layouts  6.63 us
    dot_general x1, matrix products, local(): lax.dot_general(columns, flat_out, (((0,), (0,)), ((), ())), preferred_el...  3.69 us
    dot_general x1, matrix products, local(): jnp.dot(columns, lax.all_gather(out_weight, 'dp', axis=0, tiled=True), pr...  3.15 us
    ppermute x3, starting transfers between devices, local(): lax.ppermute(ring[-1], 'tensor', [(dev, (dev + 1) % 4) for dev in range(4)])  3.08 us
  transfers between devices with their start and end apart: 7, of which 7 were waited for; matrix products, arithmetic and copies ran while one was open for 10% of the time, Pallas kernels for 0%

profile of v1, /device:TPU:0, one launch (start us, length us, event | category | flops | bytes accessed | tf_op | source)
XLA Modules:
  0.0 126.1 jit_solution(17779475500192312089)
XLA Ops:
  7.2 3.1 %collective-permute-start = (bf16[64,4096]{1,0:T(8,128)(2,1)}, bf16[64,4096]{1,0:T(8,128)(2,1)S(1)}, u32[]{:S(2)}, u32[]{:S(2)}) collective-permute-start(bf16[64,4096]{1,0:T(8,128)(2,1)} %bitcast.96), channel_id=1, source_target_pairs={{0,1},{1,2},{2,3},{3,0},{4,5},{5,6},{6,7},{7,4},{8,9},{9,10},{10,1... | collective-permute-start | bytes 1572872 | tf_op jit(solution)/shard_map/ppermute | solution.py:47
  10.3 14.2 %collective-permute-done = bf16[64,4096]{1,0:T(8,128)(2,1)S(1)} collective-permute-done((bf16[64,4096]{1,0:T(8,128)(2,1)}, bf16[64,4096]{1,0:T(8,128)(2,1)S(1)}, u32[]{:S(2)}, u32[]{:S(2)}) %collective-permute-start) | collective-permute-done | bytes 524320 | tf_op jit(solution)/shard_map/ppermute | solution.py:47
  24.5 14.9 %collective-permute-done.1 = bf16[64,4096]{1,0:T(8,128)(2,1)S(1)} collective-permute-done((bf16[64,4096]{1,0:T(8,128)(2,1)S(1)}, bf16[64,4096]{1,0:T(8,128)(2,1)S(1)}, u32[]{:S(2)}, u32[]{:S(2)}) %collective-permute-start.1) | collective-permute-done | bytes 524320 | tf_op jit(solution)/shard_map/ppermute | solution.py:47
  39.5 0.9 reshape_squeeze.3
  40.4 0.9 fusion.15
  41.3 0.4 fusion.56
  41.6 11.7 %collective-permute-done.2 = bf16[64,4096]{1,0:T(8,128)(2,1)S(1)} collective-permute-done((bf16[64,4096]{1,0:T(8,128)(2,1)S(1)}, bf16[64,4096]{1,0:T(8,128)(2,1)S(1)}, u32[]{:S(2)}, u32[]{:S(2)}) %collective-permute-start.2) | collective-permute-done | bytes 524320 | tf_op jit(solution)/shard_map/ppermute | solution.py:47
  53.4 0.8 constant_dynamic-update-slice_fusion.7
  54.2 0.8 constant_dynamic-update-slice_fusion.6
  55.0 0.9 constant_dynamic-update-slice_fusion.5
  55.9 0.8 constant_dynamic-update-slice_fusion.4
  56.7 0.8 constant_dynamic-update-slice_fusion.3
  57.6 0.8 constant_dynamic-update-slice_fusion.2
  58.4 0.8 constant_dynamic-update-slice_fusion.1
  59.2 0.8 constant_dynamic-update-slice_fusion
  60.1 8.6 %all-gather.2.cloned.1.call-done = bf16[4096,256]{1,0:T(8,128)(2,1)} async-done(((bf16[512,256]{1,0:T(8,128)(2,1)}), bf16[4096,256]{1,0:T(8,128)(2,1)}) %all-gather.2.cloned.1.call-update) | async-done | bytes 2097168 | tf_op jit(solution)/shard_map/all_gather | solution.py:56
  68.7 3.1 %fusion.12 = bf16[256,256]{0,1:T(8,128)(2,1)S(1)} fusion(bf16[4096,256]{1,0:T(8,128)(2,1)} %all-gather.2.cloned.1.call-done, bf16[512,4096]{1,0:T(8,128)(2,1)} %constant_dynamic-update-slice_fusion, s32[]{:T(128)S(6)} %select_n.19), kind=kOutput, calls=%fused_computation.17 | convolution fusion | flops 536936448 | bytes 4325380 | tf_op jit(solution)/shard_map/dot_general | solution.py:54
  71.8 0.5 multiply_reduce_fusion
  72.4 3.7 %convolution_convert_fusion = bf16[4096,256]{1,0:T(8,128)(2,1)} fusion(bf16[256,256]{0,1:T(8,128)(2,1)S(1)} %bitcast.100, bf16[512,4096]{1,0:T(8,128)(2,1)} %constant_dynamic-update-slice_fusion, s32[]{:T(128)S(6)} %select_n.19), kind=kOutput, calls=%fused_computation.1 | convolution fusion | flops 537919488 | bytes 4325380 | tf_op jit(solution)/shard_map/dot_general | solution.py:61
  76.1 0.5 fusion.66
  76.6 1.6 %collective-permute-start.4 = (bf16[256,128]{1,0:T(8,128)(2,1)S(1)}, bf16[256,128]{1,0:T(8,128)(2,1)S(1)}, u32[]{:S(2)}, u32[]{:S(2)}) collective-permute-start(bf16[256,128]{1,0:T(8,128)(2,1)S(1)} %get-tuple-element.14), channel_id=1, source_target_pairs={{0,1},{1,0},{2,3},{3,2},{4,5},{5,4},{6,7},{7,6},{8,9},{9,8},{10,11... | collective-permute-start | bytes 196616 | tf_op jit(solution)/shard_map/ppermute | solution.py:16
  78.1 0.2 fusion.11
  78.4 0.2 fusion.65
  78.6 0.2 convolution_convert_fusion.1
  78.8 0.6 collective-permute-start.3
  79.4 0.8 copy.19
  80.2 0.7 collective-permute-done.4
  80.9 0.6 fusion.20
  81.6 1.6 %collective-permute-done.3 = bf16[256,128]{1,0:T(8,128)(2,1)S(1)} collective-permute-done((bf16[256,128]{1,0:T(8,128)(2,1)S(1)}, bf16[256,128]{1,0:T(8,128)(2,1)S(1)}, u32[]{:S(2)}, u32[]{:S(2)}) %collective-permute-start.3) | collective-permute-done | bytes 65568 | tf_op jit(solution)/shard_map/ppermute | solution.py:16
  83.1 0.6 fusion.19
  83.8 33.6 %reduce-scatter.2.cloned.1.call-done = bf16[512,256]{1,0:T(8,128)(2,1)} async-done(((bf16[4096,256]{1,0:T(8,128)(2,1)}), bf16[512,256]{1,0:T(8,128)(2,1)}) %reduce-scatter.2.cloned.1.call-update) | async-done | bytes 262160 | tf_op jit(solution)/shard_map/reduce_scatter | solution.py:60
  117.4 1.8 %convert_multiply_fusion = f32[512,256]{1,0:T(8,128)} fusion(bf16[512,256]{1,0:T(8,128)(2,1)} %reduce-scatter.2.cloned.1.call-done), kind=kLoop, calls=%fused_computation.20 | loop fusion | flops 262144 | bytes 786432 | tf_op jit(solution)/shard_map/div | solution.py:92
  (12 shorter events, 0.1 us)
Async XLA Ops:
  7.2 34.1 %copy-start = (bf16[1,256,128]{2,1,0:T(8,128)(2,1)S(1)}, bf16[1,256,128]{2,1,0:T(8,128)(2,1)}, u32[]{:S(2)}) copy-start(bf16[1,256,128]{2,1,0:T(8,128)(2,1)} %param.9) | copy-start | bytes 196612
  7.2 48.7 %copy-start.1 = (bf16[1,64,4096]{2,1,0:T(8,128)(2,1)S(1)}, bf16[1,64,4096]{2,1,0:T(8,128)(2,1)}, u32[]{:S(2)}) copy-start(bf16[1,64,4096]{2,1,0:T(8,128)(2,1)} %param.6) | copy-start | bytes 1572868
  7.2 61.5 %all-gather.2.cloned.1.call-start = ((), (), s32[]{:S(2)}) async-start(), calls=%async_computation.1 | async-start | bytes 2359296 | tf_op jit(solution)/shard_map/all_gather | solution.py:56
  7.2 17.2 %collective-permute-start = (bf16[64,4096]{1,0:T(8,128)(2,1)}, bf16[64,4096]{1,0:T(8,128)(2,1)S(1)}, u32[]{:S(2)}, u32[]{:S(2)}) collective-permute-start(bf16[64,4096]{1,0:T(8,128)(2,1)} %bitcast.96), channel_id=1, source_target_pairs={{0,1},{1,2},{2,3},{3,0},{4,5},{5,6},{6,7},{7,4},{8,9},{9,10},{10,1... | collective-permute-start | bytes 1572872 | tf_op jit(solution)/shard_map/ppermute | solution.py:47
  24.5 14.9 %collective-permute-start.1 = (bf16[64,4096]{1,0:T(8,128)(2,1)S(1)}, bf16[64,4096]{1,0:T(8,128)(2,1)S(1)}, u32[]{:S(2)}, u32[]{:S(2)}) collective-permute-start(bf16[64,4096]{1,0:T(8,128)(2,1)S(1)} %collective-permute-done), channel_id=1, source_target_pairs={{0,1},{1,2},{2,3},{3,0},{4,5},{5,6},{6,7},{7,4},{8,9},{9,10},{10,1... | collective-permute-start | bytes 1572872 | tf_op jit(solution)/shard_map/ppermute | solution.py:47
  39.4 14.0 %collective-permute-start.2 = (bf16[64,4096]{1,0:T(8,128)(2,1)S(1)}, bf16[64,4096]{1,0:T(8,128)(2,1)S(1)}, u32[]{:S(2)}, u32[]{:S(2)}) collective-permute-start(bf16[64,4096]{1,0:T(8,128)(2,1)S(1)} %collective-permute-done.1), channel_id=1, source_target_pairs={{0,1},{1,2},{2,3},{3,0},{4,5},{5,6},{6,7},{7,4},{8,9},{9,10},{10,1... | collective-permute-start | bytes 1572872 | tf_op jit(solution)/shard_map/ppermute | solution.py:47
  39.4 78.0 %reduce-scatter.2.cloned.1.call-start = ((), (), s32[]{:S(2)}) async-start(), calls=%async_computation.2 | async-start | bytes 2359296 | tf_op jit(solution)/shard_map/reduce_scatter | solution.py:60
  56.7 15.1 %copy-start.2 = (bf16[1,256,128]{2,1,0:T(8,128)(2,1)S(1)}, bf16[1,256,128]{2,1,0:T(8,128)(2,1)}, u32[]{:S(2)}) copy-start(bf16[1,256,128]{2,1,0:T(8,128)(2,1)} %param.10) | copy-start | bytes 196612
  76.6 4.3 %collective-permute-start.4 = (bf16[256,128]{1,0:T(8,128)(2,1)S(1)}, bf16[256,128]{1,0:T(8,128)(2,1)S(1)}, u32[]{:S(2)}, u32[]{:S(2)}) collective-permute-start(bf16[256,128]{1,0:T(8,128)(2,1)S(1)} %get-tuple-element.14), channel_id=1, source_target_pairs={{0,1},{1,0},{2,3},{3,2},{4,5},{5,4},{6,7},{7,6},{8,9},{9,8},{10,11... | collective-permute-start | bytes 196616 | tf_op jit(solution)/shard_map/ppermute | solution.py:16
  78.8 4.3 %collective-permute-start.3 = (bf16[256,128]{1,0:T(8,128)(2,1)S(1)}, bf16[256,128]{1,0:T(8,128)(2,1)S(1)}, u32[]{:S(2)}, u32[]{:S(2)}) collective-permute-start(bf16[256,128]{1,0:T(8,128)(2,1)S(1)} %get-tuple-element.12), channel_id=1, source_target_pairs={{0,1},{1,0},{2,3},{3,2},{4,5},{5,4},{6,7},{7,6},{8,9},{9,8},{10,11... | collective-permute-start | bytes 196616 | tf_op jit(solution)/shard_map/ppermute | solution.py:16
Sparse Core Ops, SparseCore 0:
  39.5 29.1 all-gather.1
  76.2 41.1 reduce-scatter.1
